TPU v7x, 32 devices: a whole 2x2x4 slice. The times are simulated.
32 devices in a mesh: tile: 16 (over z, x, core), build: 2 (over y).
Axes of the slice: x: 2, y: 2, z: 4, core: 2. Of those that a mesh axis runs over, the one named last changes fastest.
Arguments:
- loads: float32 [8, 3, 128, 128], P('build', None, 'tile'), may hold values from -4 to 4
- guess: float32 [8, 3, 128, 128], P('build', None, 'tile'), may hold values from -0.6 to 0.6
- material: int32 [8, 128, 128], P('build', 'tile'), may hold values from 0 to 1
- clamped: int32 [8, 128, 128], P('build', 'tile'), may hold values 0 or 1
- moduli: float32 [2], replicated, may hold values from 0.3 to 3
Outputs:
- distortion: float32 [8, 3, 128, 128], P('build', None, 'tile')
- imbalance: float32 [8, 3, 128, 128], P('build', None, 'tile')
Inputs may be any that keep to these rules, and one draw needn't show every extreme that they name: `material`: 0 marks a support element, 1 a part element.
All inputs are finite; a program needn't handle non-finite values. No bound on the sum of `clamped` on one device may be relied on, other than what follows from the above.
Results may differ from a plain program's by a relative error of at most 0.0003.
Values sent between devices are 32-bit elements; how exact they have to be, the bound alone decides.
A program may use at most 64 MiB of HBM per device.

v0:
```python
import math

import jax
import jax.numpy as jnp
import numpy as np
from jax import lax
from jax.sharding import PartitionSpec as P

SWEEPS = 2


relax_shifts = (0.0, 0.05, 0.2)
relax_weights = (0.5, 0.3, 0.2)


def passed_along(block, axis, distance):
    devices = range(lax.axis_size(axis))
    route = [(i - distance, i) for i in devices if i - distance in devices]
    return lax.ppermute(block, axis, route)


def extended_2(shard, sides, width):
    for axis, dim in sides:
        count, length = (lax.axis_size(axis), shard.shape[dim])
        up = [(i, (i + 1) % count) for i in range(count - 1)]
        down = [(j, i) for i, j in up]
        last = lax.slice_in_dim(shard, length - width, length, axis=dim)
        leading = lax.slice_in_dim(shard, 0, width, axis=dim)
        before = lax.ppermute(last, axis, up)
        after = lax.ppermute(leading, axis, down)
        shard = jnp.concatenate([before, shard, after], axis=dim)
    return shard


def carried_in(part, axis, combine, identity, reverse):
    count = lax.axis_size(axis)
    place = lax.axis_index(axis)
    ahead = count - 1 - place if reverse else place
    gathered = jax.tree.map(lambda a: lax.all_gather(a, axis), part)
    state = jax.tree.map(lambda a, e: jnp.zeros_like(a) + jnp.asarray(e, a.dtype), part, identity)

    def one(step, state):
        source = count - 1 - step if reverse else step
        return combine(
            state, jax.tree.map(lambda a: lax.dynamic_index_in_dim(a, source, 0, False), gathered)
        )

    return lax.fori_loop(0, ahead, one, state)


def element_matrix():
    spacing = np.array([1.0, 8.0, 8.0])
    poisson = 0.3
    lame_first = poisson / ((1.0 + poisson) * (1.0 - 2.0 * poisson))
    lame_second = 0.5 / (1.0 + poisson)
    elastic = np.zeros((6, 6))
    elastic[:3, :3] = lame_first
    for entry in range(3):
        elastic[entry, entry] += 2.0 * lame_second
        elastic[3 + entry, 3 + entry] = lame_second
    points = (0.5 - 0.5 / math.sqrt(3.0), 0.5 + 0.5 / math.sqrt(3.0))
    matrix = np.zeros((24, 24))
    volume = float(np.prod(spacing)) / 8.0
    for point_z in points:
        for point_x in points:
            for point_y in points:
                position = (point_z, point_x, point_y)
                strain = np.zeros((6, 24))
                for corner in range(8):
                    upper_side = (corner >> 2 & 1, corner >> 1 & 1, corner & 1)
                    values = [
                        position[direction] if upper_side[direction] else 1.0 - position[direction]
                        for direction in range(3)
                    ]
                    slopes = [
                        (1.0 if upper_side[direction] else -1.0) / spacing[direction]
                        for direction in range(3)
                    ]
                    gradient = [
                        slopes[0] * values[1] * values[2],
                        values[0] * slopes[1] * values[2],
                        values[0] * values[1] * slopes[2],
                    ]
                    column = 3 * corner
                    strain[0, column] = gradient[0]
                    strain[1, column + 1] = gradient[1]
                    strain[2, column + 2] = gradient[2]
                    strain[3, column] = gradient[1]
                    strain[3, column + 1] = gradient[0]
                    strain[4, column + 1] = gradient[2]
                    strain[4, column + 2] = gradient[1]
                    strain[5, column] = gradient[2]
                    strain[5, column + 2] = gradient[0]
                matrix += strain.T @ elastic @ strain * volume
    largest = 0.0
    for entry in range(24):
        largest = largest if largest >= float(matrix[entry, entry]) else float(matrix[entry, entry])
    return matrix / largest


def corner_steps(corner):
    return (corner >> 2 & 1, corner >> 1 & 1, corner & 1)


def element_forces(extended, moduli_ext, stiffness):
    depth = extended.shape[0] - 2
    width = extended.shape[2] - 2
    length = extended.shape[3] - 2
    pieces = []
    for corner in range(8):
        step_z, step_x, step_y = corner_steps(corner)
        pieces.append(
            extended[
                step_z : step_z + depth + 1,
                :,
                step_x : step_x + width + 1,
                step_y : step_y + length + 1,
            ]
        )
    stacked = jnp.concatenate(pieces, axis=1)
    forces = jnp.einsum("ij,zjxy->zixy", stiffness, stacked, precision=lax.Precision.HIGHEST)
    forces = forces * moduli_ext[:, None]
    summed = jnp.zeros((depth, 3, width, length), jnp.float32)
    for corner in range(8):
        step_z, step_x, step_y = corner_steps(corner)
        summed = (
            summed
            + forces[
                1 - step_z : 1 - step_z + depth,
                3 * corner : 3 * corner + 3,
                1 - step_x : 1 - step_x + width,
                1 - step_y : 1 - step_y + length,
            ]
        )
    return summed


def line_blocks(moduli_ext, free, stiffness):
    depth, width, length = free.shape
    diagonal = jnp.zeros((depth, 3, 3, width, length), jnp.float32)
    for corner in range(8):
        step_z, step_x, step_y = corner_steps(corner)
        sub_block = stiffness[3 * corner : 3 * corner + 3, 3 * corner : 3 * corner + 3]
        weight = moduli_ext[
            1 - step_z : 1 - step_z + depth,
            1 - step_x : 1 - step_x + width,
            1 - step_y : 1 - step_y + length,
        ]
        diagonal = diagonal + sub_block[None, :, :, None, None] * weight[:, None, None]
    upper_blocks = jnp.zeros((depth + 1, 3, 3, width, length), jnp.float32)
    for corner in range(4):
        step_x, step_y = (corner >> 1, corner & 1)
        sub_block = stiffness[3 * corner : 3 * corner + 3, 3 * corner + 12 : 3 * corner + 15]
        weight = moduli_ext[:, 1 - step_x : 1 - step_x + width, 1 - step_y : 1 - step_y + length]
        upper_blocks = upper_blocks + sub_block[None, :, :, None, None] * weight[:, None, None]
    identity = jnp.eye(3, dtype=jnp.float32)[None, :, :, None, None]
    free_rows = free[:, None, None]
    diagonal = free_rows * diagonal + (1.0 - free_rows) * identity
    above = free_rows * upper_blocks[1:]
    below = free_rows * jnp.swapaxes(upper_blocks[:-1], 1, 2)
    return (diagonal, below, above)


def apply(matrix, other):
    extra = other.ndim - matrix.ndim + 1
    summed = None
    for entry in range(3):
        left = matrix[:, entry]
        left = left.reshape(left.shape[:1] + (1,) * extra + left.shape[1:])
        product = left * other[entry]
        summed = product if summed is None else summed + product
    return summed


def apply_nodes(spikes, vector):
    summed = None
    for entry in range(3):
        product = spikes[:, :, entry] * vector[entry][None]
        summed = product if summed is None else summed + product
    return summed


def invert(matrix):
    entries = [[matrix[row_index, col_index] for col_index in range(3)] for row_index in range(3)]

    def cofactor(row_index, col_index):
        return (
            entries[(row_index + 1) % 3][(col_index + 1) % 3]
            * entries[(row_index + 2) % 3][(col_index + 2) % 3]
            - entries[(row_index + 1) % 3][(col_index + 2) % 3]
            * entries[(row_index + 2) % 3][(col_index + 1) % 3]
        )

    determinant = (
        entries[0][0] * cofactor(0, 0)
        + entries[0][1] * cofactor(0, 1)
        + entries[0][2] * cofactor(0, 2)
    )
    rows_out = [
        jnp.stack([cofactor(col_index, row_index) / determinant for col_index in range(3)])
        for row_index in range(3)
    ]
    return jnp.stack(rows_out)


def factorize(scaled, below, above):

    def eliminate(previous, inputs):
        pivot_block, below_block, above_block = inputs
        inverse = invert(pivot_block - apply(below_block, previous))
        couple = apply(inverse, above_block)
        return (couple, (inverse, couple))

    initial = jnp.zeros(scaled.shape[1:], jnp.float32)
    unused, (inverses, couples) = lax.scan(eliminate, initial, (scaled, below, above))
    return (inverses, couples)


def substitute(inverses, couples, below, right_side):

    def forward(previous, inputs):
        inverse, below_block, right_block = inputs
        current = apply(inverse, right_block - apply(below_block, previous))
        return (current, current)

    initial = jnp.zeros(right_side.shape[1:], jnp.float32)
    unused, eliminated = lax.scan(forward, initial, (inverses, below, right_side))

    def backward(following, inputs):
        couple, current = inputs
        solved = current - apply(couple, following)
        return (solved, solved)

    unused, solution = lax.scan(backward, initial, (couples, eliminated), reverse=True)
    return solution


def widen(values, place_at, count):
    expanded = jnp.expand_dims(values, place_at)
    target = expanded.shape[:place_at] + (count,) + expanded.shape[place_at + 1 :]
    return jnp.broadcast_to(expanded, target)


def interface_terms(previous, spike_ends, identity):
    top_upper, bottom_upper, top_lower, bottom_lower = spike_ends
    coupled = invert(identity - apply(top_lower, previous))
    carry_top = apply(coupled, top_upper)
    scaled_lower = apply(apply(bottom_lower, previous), coupled)
    next_block = bottom_upper + apply(scaled_lower, top_upper)
    forward_map = -bottom_lower - apply(scaled_lower, top_lower)
    return (next_block, (coupled, carry_top, scaled_lower, forward_map))


def compose(earlier, later):
    return (apply(later[0], earlier[0]), apply(later[0], earlier[1]) + later[1])


def on_device(loads, guess, material, clamped, moduli):
    stiffness = jnp.asarray(element_matrix(), jnp.float32)
    layers = lax.axis_size("build")
    layer_index = lax.axis_index("build")
    free = (1 - clamped).astype(jnp.float32)
    modulus = jnp.where(material == 1, moduli[1], moduli[0])
    rim_layer = passed_along(modulus[-1:], "build", 1)
    layered = jnp.concatenate([rim_layer, modulus], axis=0)
    rim_column = passed_along(layered[:, -1:], "tile", 1)
    moduli_ext = jnp.concatenate([rim_column, layered], axis=1)
    moduli_ext = jnp.pad(moduli_ext, ((0, 0), (0, 0), (1, 0)))
    diagonal, below, above = line_blocks(moduli_ext, free, stiffness)
    factors = 1.0 + jnp.asarray(relax_shifts, jnp.float32)
    weights = jnp.asarray(relax_weights, jnp.float32)
    count = len(relax_shifts)

    def residual_of(field):
        extended = extended_2(field, (("tile", 2), ("build", 0)), 1)
        extended = jnp.pad(extended, ((0, 0), (0, 0), (0, 0), (1, 1)))
        return free[:, None] * (loads - element_forces(extended, moduli_ext, stiffness))

    spike_top = above[-1] * (layer_index < layers - 1).astype(jnp.float32)
    spike_bottom = below[0]
    inner_below = below.at[0].set(0.0)
    inner_above = above.at[-1].set(0.0)
    scaled = diagonal[:, :, :, None] * factors[:, None, None]
    below_wide = widen(inner_below, 3, count)
    inverses, couples = factorize(scaled, below_wide, widen(inner_above, 3, count))
    blank = jnp.zeros(scaled.shape, jnp.float32)
    top_source = blank.at[-1].set(widen(spike_top, 2, count))
    bottom_source = blank.at[0].set(widen(spike_bottom, 2, count))
    upper_spike = substitute(inverses, couples, below_wide, top_source)
    lower_spike = substitute(inverses, couples, below_wide, bottom_source)
    spike_ends = (upper_spike[0], upper_spike[-1], lower_spike[0], lower_spike[-1])
    identity = jnp.broadcast_to(
        jnp.eye(3, dtype=jnp.float32)[:, :, None, None, None], spike_ends[0].shape
    )
    zero_vector = jnp.zeros(spike_ends[0].shape[1:], jnp.float32)

    def chain_turn(turn_index, previous):
        next_block, terms = interface_terms(previous, spike_ends, identity)
        return passed_along(next_block, "build", 1)

    prev_block = lax.fori_loop(0, layers - 1, chain_turn, jnp.zeros_like(identity))
    unused, (coupled, carry_top, scaled_lower, forward_map) = interface_terms(
        prev_block, spike_ends, identity
    )
    displacement = guess
    for sweep_index in range(SWEEPS):
        relax_local = substitute(
            inverses, couples, below_wide, widen(residual_of(displacement), 2, count)
        )
        top_end = relax_local[0]
        bottom_end = relax_local[-1]
        source = bottom_end + apply(scaled_lower, top_end)
        unused_a, prev_value = carried_in(
            (forward_map, source), "build", compose, (identity, zero_vector), False
        )
        offset_top = apply(coupled, top_end - apply(spike_ends[2], prev_value))
        unused_b, relax_next_top = carried_in(
            (-carry_top, offset_top), "build", compose, (identity, zero_vector), True
        )
        own_top = offset_top - apply(carry_top, relax_next_top)
        relax_prev_bottom = prev_value - apply(prev_block, own_top)
        solved = (
            relax_local
            - apply_nodes(upper_spike, relax_next_top)
            - apply_nodes(lower_spike, relax_prev_bottom)
        )
        displacement = displacement + jnp.sum(solved * weights[:, None, None], axis=2)
    return (displacement, residual_of(displacement))


def solution(mesh):
    return jax.shard_map(
        on_device,
        mesh=mesh,
        in_specs=(
            P("build", None, "tile", None),
            P("build", None, "tile", None),
            P("build", "tile", None),
            P("build", "tile", None),
            P(),
        ),
        out_specs=(P("build", None, "tile", None), P("build", None, "tile", None)),
        check_vma=False,
    )
```

profile of v0, /device:TPU:1, one launch (start us, length us, event | category | flops | bytes accessed | tf_op | source)
XLA Modules:
  0.0 150.0 jit_solution(4637773424734678529)
XLA Ops:
  0.7 1.3 fusion.98
  2.0 2.0 %compare_select_fusion = f32[4,8,128]{2,1,0:T(8,128)S(1)} fusion(s32[4,8,128]{2,1,0:T(8,128)} %param.44, f32[]{:T(128)} %bitcast.33, f32[]{:T(128)} %bitcast.32), kind=kLoop, calls=%fused_computation.417 | loop fusion | flops 8192 | bytes 32776 | tf_op jit(solution)/shard_map/jit(_where)/select_n | solution.py:263
  4.0 4.0 %collective-permute-start = (f32[1,8,128]{2,1,0:T(8,128)S(1)}, f32[1,8,128]{2,1,0:T(8,128)S(1)}, u32[]{:S(2)}, u32[]{:S(2)}) collective-permute-start(f32[1,8,128]{2,1,0:T(8,128)S(1)} %slice.1784), channel_id=1, source_target_pairs={{0,1},{2,3},{4,5},{6,7},{8,9},{10,11},{12,13},{14,15},{16,17},{18,... | collective-permute-start | bytes 12296 | tf_op jit(solution)/shard_map/ppermute | solution.py:19
  8.0 0.9 fusion.97
  8.9 4.0 %collective-permute-start.2 = (f32[4,3,1,128]{3,1,2,0:T(4,128)S(1)}, f32[4,3,1,128]{3,1,2,0:T(4,128)S(1)}, u32[]{:S(2)}, u32[]{:S(2)}) collective-permute-start(f32[4,3,1,128]{3,1,2,0:T(4,128)S(1)} %copy.124), channel_id=1, source_target_pairs={{0,2},{2,4},{4,6},{6,8},{8,10},{10,12},{12,14},{14,16},{16,18},{18... | collective-permute-start | bytes 18440 | tf_op jit(solution)/shard_map/ppermute | solution.py:29
  12.9 1.9 %collective-permute-start.3 = (f32[4,3,1,128]{3,1,2,0:T(4,128)S(1)}, f32[4,3,1,128]{3,1,2,0:T(4,128)S(1)}, u32[]{:S(2)}, u32[]{:S(2)}) collective-permute-start(f32[4,3,1,128]{3,1,2,0:T(4,128)S(1)} %copy.125), channel_id=1, source_target_pairs={{2,0},{4,2},{6,4},{8,6},{10,8},{12,10},{14,12},{16,14},{18,16},{20... | collective-permute-start | bytes 18440 | tf_op jit(solution)/shard_map/ppermute | solution.py:30
  14.8 0.7 subtract_convert_fusion
  15.5 0.7 broadcast_subtract_fusion.1
  16.4 3.6 %collective-permute-start.1 = (f32[5,1,128]{2,1,0:T(1,128)S(1)}, f32[5,1,128]{2,1,0:T(1,128)S(1)}, u32[]{:S(2)}, u32[]{:S(2)}) collective-permute-start(f32[5,1,128]{2,1,0:T(1,128)S(1)} %fusion.83), channel_id=1, source_target_pairs={{0,2},{2,4},{4,6},{6,8},{8,10},{10,12},{12,14},{14,16},{16,18},{18... | collective-permute-start | bytes 7688 | tf_op jit(solution)/shard_map/ppermute | solution.py:19
  20.1 0.8 constant_dynamic-update-slice_fusion.1
  21.5 1.3 collective-permute-start.4
  22.8 1.3 collective-permute-start.5
  24.3 0.8 multiply_add_fusion.5
  25.7 1.6 %while.199 = (s32[]{:T(128)}, f32[3,3,3,8,128]{4,3,2,1,0:T(8,128)S(1)}, f32[4,3,3,3,8,128]{5,4,3,1,2,0:T(8,128)S(1)}, f32[4,3,3,3,8,128]{5,4,3,1,2,0:T(8,128)S(1...) while((s32[]{:T(128)}, ...), condition=%wide.region_1.2_spmd.clone, body=%wide.region_0.1_spmd.clone.sunk | while | flops 706565 | bytes 3686567 | solution.py:215
  27.3 1.0 while.204
  28.4 0.7 while.205
  29.2 0.6 slice_bitcast_fusion.131
  29.9 0.6 slice_bitcast_fusion.128
  30.6 0.6 slice_bitcast_fusion.125
  31.4 1.0 while.202
  32.4 0.7 while.203
  33.2 0.7 fusion.66
  33.9 0.6 slice_bitcast_fusion.135
  34.5 5.2 %collective-permute-start.6 = (f32[3,3,3,8,128]{4,3,2,0,1:T(8,128)}, f32[3,3,3,8,128]{4,3,2,0,1:T(8,128)}, u32[]{:S(2)}, u32[]{:S(2)}) collective-permute-start(f32[3,3,3,8,128]{4,3,2,0,1:T(8,128)} %fusion.66), channel_id=1, source_target_pairs={{0,1},{2,3},{4,5},{6,7},{8,9},{10,11},{12,13},{14,15},{16,17},{18,... | collective-permute-start | bytes 331784 | tf_op jit(solution)/shard_map/while/body/eval_jaxpr/ppermute | solution.py:19
  39.9 0.9 select_maximum_fusion.8
  40.8 1.6 %fusion.93 = (f32[5,3,9,129]{3,1,2,0:T(4,128)}, f32[5,3,9,129]{3,1,2,0:T(4,128)}, f32[5,3,9,129]{3,1,2,0:T(4,128)}, f32[5,3,9,129]{3,1,2,0:T(4,128)}, f32[5,3,9,...) fusion(f32[6,3,10,130]{3,1,2,0:T(4,128)S(1)} %select_maximum_fusion.8), kind=kLoop, calls=%fused_computation.507 | loop fusion | bytes 1114560 | tf_op jit(solution)/shard_map/slice | solution.py:113
  42.3 9.2 %concatenate.45 = f32[5,24,9,129]{3,1,2,0:T(8,128)S(1)} concatenate(f32[5,3,9,129]{3,1,2,0:T(4,128)} %get-tuple-element.1482, f32[5,3,9,129]{3,1,2,0:T(4,128)} %get-tuple-element.1481, f32[5,3,9,129]{3,1,2,0:T(4,128)} %get-tuple-element.1480, f32[5,3,9,129]{3,1,2,0:T(4,128)} %get-tuple-element.1479, f32[5,3,9,129]{3,1,2,0:T(4,128)} %get-tuple-element.1478, ...), dimensions={1} | concatenate | bytes 1114560 | tf_op jit(solution)/shard_map/concatenate | solution.py:120
  51.5 1.8 %fusion.63 = f32[5,24,9,129]{3,1,2,0:T(8,128)S(1)} fusion(f32[5,24,9,129]{3,1,2,0:T(8,128)S(1)} %concatenate.45, f32[24,24,1,1]{1,0,3,2:T(8,128)} %constant.436, f32[5,9,129]{2,1,0:T(8,128)S(1)} %pad.24), kind=kOutput, calls=%fused_computation.254 | convolution fusion | flops 40263480 | bytes 1140084 | tf_op jit(solution)/shard_map/ij,zjxy->zixy/dot_general | solution.py:121
  55.4 0.8 slice_bitcast_fusion.122
  56.6 0.7 add_negate_fusion
  57.4 3.8 %all_gather.14 = f32[2,3,3,8,128]{4,3,2,1,0:T(8,128)S(1)} all-gather(f32[1,3,3,8,128]{4,3,2,1,0:T(8,128)S(1)} %fusion.77), channel_id=1, replica_groups=mesh['tile'=16,'build'=2] {'build'}, dimensions={0}, use_global_device_ids=true | all-gather | bytes 110592 | tf_op jit(solution)/shard_map/all_gather | solution.py:39
  61.2 4.9 %all_gather.13 = f32[2,3,3,3,8,128]{5,4,3,2,1,0:T(8,128)S(1)} all-gather(f32[1,3,3,3,8,128]{5,4,3,2,1,0:T(8,128)S(1)} %add_subtract_fusion), channel_id=1, replica_groups=mesh['tile'=16,'build'=2] {'build'}, dimensions={0}, use_global_device_ids=true | all-gather | bytes 331776 | tf_op jit(solution)/shard_map/all_gather | solution.py:39
  66.2 3.5 %all_gather.15 = f32[2,3,3,8,128]{4,3,2,1,0:T(8,128)S(1)} all-gather(f32[1,3,3,8,128]{4,3,2,1,0:T(8,128)S(1)} %fusion.72), channel_id=1, replica_groups=mesh['tile'=16,'build'=2] {'build'}, dimensions={0}, use_global_device_ids=true | all-gather | bytes 110592 | tf_op jit(solution)/shard_map/all_gather | solution.py:39
  69.7 4.5 %all_gather.12 = f32[2,3,3,3,8,128]{5,4,3,2,1,0:T(8,128)S(1)} all-gather(f32[1,3,3,3,8,128]{5,4,3,2,1,0:T(8,128)} %add_negate_fusion), channel_id=1, replica_groups=mesh['tile'=16,'build'=2] {'build'}, dimensions={0}, use_global_device_ids=true | all-gather | bytes 331776 | tf_op jit(solution)/shard_map/all_gather | solution.py:39
  74.4 0.8 add_subtract_fusion.4
  75.4 7.2 %collective-permute-start.7 = (f32[4,3,1,128]{3,1,2,0:T(4,128)S(1)}, f32[4,3,1,128]{3,1,2,0:T(4,128)S(1)}, u32[]{:S(2)}, u32[]{:S(2)}) collective-permute-start(f32[4,3,1,128]{3,1,2,0:T(4,128)S(1)} %get-tuple-element.1538), channel_id=1, source_target_pairs={{0,2},{2,4},{4,6},{6,8},{8,10},{10,12},{12,14},{14,16},{16,18},{18... | collective-permute-start | bytes 18440 | tf_op jit(solution)/shard_map/ppermute | solution.py:29
  82.6 1.9 %collective-permute-start.8 = (f32[4,3,1,128]{3,1,2,0:T(4,128)S(1)}, f32[4,3,1,128]{3,1,2,0:T(4,128)S(1)}, u32[]{:S(2)}, u32[]{:S(2)}) collective-permute-start(f32[4,3,1,128]{3,1,2,0:T(4,128)S(1)} %get-tuple-element.1539), channel_id=1, source_target_pairs={{2,0},{4,2},{6,4},{8,6},{10,8},{12,10},{14,12},{16,14},{18,16},{20... | collective-permute-start | bytes 18440 | tf_op jit(solution)/shard_map/ppermute | solution.py:30
  84.5 3.0 %collective-permute-done.8 = f32[4,3,1,128]{3,1,2,0:T(4,128)S(1)} collective-permute-done((f32[4,3,1,128]{3,1,2,0:T(4,128)S(1)}, f32[4,3,1,128]{3,1,2,0:T(4,128)S(1)}, u32[]{:S(2)}, u32[]{:S(2)}) %collective-permute-start.8) | collective-permute-done | bytes 6176 | tf_op jit(solution)/shard_map/ppermute | solution.py:30
  87.6 1.3 collective-permute-start.10
  88.9 4.0 %collective-permute-start.9 = (f32[1,3,10,128]{3,1,2,0:T(4,128)S(1)}, f32[1,3,10,128]{3,1,2,0:T(4,128)S(1)}, u32[]{:S(2)}, u32[]{:S(2)}) collective-permute-start(f32[1,3,10,128]{3,1,2,0:T(4,128)S(1)} %get-tuple-element.1532), channel_id=1, source_target_pairs={{0,1},{2,3},{4,5},{6,7},{8,9},{10,11},{12,13},{14,15},{16,17},{18,... | collective-permute-start | bytes 46088 | tf_op jit(solution)/shard_map/ppermute | solution.py:29
  92.9 0.9 collective-permute-done.9
  94.0 1.4 fusion.92
  95.4 14.2 %concatenate.48 = f32[5,24,9,129]{3,1,2,0:T(8,128)} concatenate(f32[5,3,9,129]{3,1,2,0:T(4,128)} %get-tuple-element.1474, f32[5,3,9,129]{3,1,2,0:T(4,128)} %get-tuple-element.1473, f32[5,3,9,129]{3,1,2,0:T(4,128)} %get-tuple-element.1472, f32[5,3,9,129]{3,1,2,0:T(4,128)} %get-tuple-element.1471, f32[5,3,9,129]{3,1,2,0:T(4,128)} %get-tuple-element.1470, ...), dimensions={1} | concatenate | bytes 1114560 | tf_op jit(solution)/shard_map/concatenate | solution.py:120
  109.6 2.3 %fusion.62 = f32[5,24,9,129]{3,1,2,0:T(8,128)S(1)} fusion(f32[5,24,9,129]{3,1,2,0:T(8,128)} %concatenate.48, f32[24,24,1,1]{1,0,3,2:T(8,128)S(1)} %copy-done.29, f32[5,9,129]{2,1,0:T(8,128)S(1)} %pad.24), kind=kOutput, calls=%fused_computation.252 | convolution fusion | flops 40263480 | bytes 1140084 | tf_op jit(solution)/shard_map/ij,zjxy->zixy/dot_general | solution.py:121
  112.2 0.7 broadcast_in_dim.45
  112.9 3.7 %while.206 = (s32[]{:T(128)}, f32[3,3,8,128]{3,2,1,0:T(8,128)S(1)}, f32[4,3,3,8,128]{4,3,2,1,0:T(8,128)S(1)}, f32[4,3,3,3,8,128]{5,4,3,1,2,0:T(8,128)S(1)}, f32[...) while((s32[]{:T(128)}, f32[3,3,8,128]{3,2,1,0:T(8,128)S(1)}, ...), condition=%wide.region_20.21_spmd.clone, body=%wide.region_19.20_spmd.clone.sunk | while | flops 156675 | bytes 1253483 | solution.py:227
  113.0 0.8 fusion.138
  113.9 0.8 fusion.138
  114.8 0.8 fusion.138
  115.8 0.8 fusion.138
  117.2 3.9 %all_gather.32 = f32[2,3,3,8,128]{4,3,2,1,0:T(8,128)S(1)} all-gather(f32[1,3,3,8,128]{4,3,2,1,0:T(8,128)S(1)} %fusion.79), channel_id=1, replica_groups=mesh['tile'=16,'build'=2] {'build'}, dimensions={0}, use_global_device_ids=true | all-gather | bytes 110592 | tf_op jit(solution)/shard_map/all_gather | solution.py:39
  121.1 4.1 %all_gather.33 = f32[2,3,3,8,128]{4,3,2,1,0:T(8,128)S(1)} all-gather(f32[1,3,3,8,128]{4,3,2,1,0:T(8,128)S(1)} %fusion.73), channel_id=1, replica_groups=mesh['tile'=16,'build'=2] {'build'}, dimensions={0}, use_global_device_ids=true | all-gather | bytes 110592 | tf_op jit(solution)/shard_map/all_gather | solution.py:39
  125.3 0.8 copy-done.3
  126.1 0.8 add_subtract_fusion.2
  127.1 5.1 %collective-permute-start.11 = (f32[4,3,1,128]{3,1,2,0:T(4,128)S(1)}, f32[4,3,1,128]{3,1,2,0:T(4,128)S(1)}, u32[]{:S(2)}, u32[]{:S(2)}) collective-permute-start(f32[4,3,1,128]{3,1,2,0:T(4,128)S(1)} %get-tuple-element.1536), channel_id=1, source_target_pairs={{0,2},{2,4},{4,6},{6,8},{8,10},{10,12},{12,14},{14,16},{16,18},{18... | collective-permute-start | bytes 18440 | tf_op jit(solution)/shard_map/ppermute | solution.py:29
  132.2 1.9 %collective-permute-start.12 = (f32[4,3,1,128]{3,1,2,0:T(4,128)S(1)}, f32[4,3,1,128]{3,1,2,0:T(4,128)S(1)}, u32[]{:S(2)}, u32[]{:S(2)}) collective-permute-start(f32[4,3,1,128]{3,1,2,0:T(4,128)S(1)} %get-tuple-element.1537), channel_id=1, source_target_pairs={{2,0},{4,2},{6,4},{8,6},{10,8},{12,10},{14,12},{16,14},{18,16},{20... | collective-permute-start | bytes 18440 | tf_op jit(solution)/shard_map/ppermute | solution.py:30
  134.2 3.0 %collective-permute-done.12 = f32[4,3,1,128]{3,1,2,0:T(4,128)S(1)} collective-permute-done((f32[4,3,1,128]{3,1,2,0:T(4,128)S(1)}, f32[4,3,1,128]{3,1,2,0:T(4,128)S(1)}, u32[]{:S(2)}, u32[]{:S(2)}) %collective-permute-start.12) | collective-permute-done | bytes 6176 | tf_op jit(solution)/shard_map/ppermute | solution.py:30
  137.2 3.7 %collective-permute-start.13 = (f32[1,3,10,128]{3,1,2,0:T(4,128)S(1)}, f32[1,3,10,128]{3,1,2,0:T(4,128)S(1)}, u32[]{:S(2)}, u32[]{:S(2)}) collective-permute-start(f32[1,3,10,128]{3,1,2,0:T(4,128)S(1)} %get-tuple-element.1530), channel_id=1, source_target_pairs={{0,1},{2,3},{4,5},{6,7},{8,9},{10,11},{12,13},{14,15},{16,17},{18,... | collective-permute-start | bytes 46088 | tf_op jit(solution)/shard_map/ppermute | solution.py:29
  140.9 1.5 collective-permute-start.14
  142.4 0.6 copy.88
  143.0 2.4 %collective-permute-done.14 = f32[1,3,10,128]{3,1,2,0:T(4,128)S(1)} collective-permute-done((f32[1,3,10,128]{3,1,2,0:T(4,128)S(1)}, f32[1,3,10,128]{3,1,2,0:T(4,128)S(1)}, u32[]{:S(2)}, u32[]{:S(2)}) %collective-permute-start.14) | collective-permute-done | bytes 15392 | tf_op jit(solution)/shard_map/ppermute | solution.py:30
  146.1 2.0 %concatenate.51 = f32[5,24,9,129]{3,1,2,0:T(8,128)S(1)} concatenate(f32[5,3,9,129]{3,1,2,0:T(4,128)S(1)} %get-tuple-element.1466, f32[5,3,9,129]{3,1,2,0:T(4,128)S(1)} %get-tuple-element.1465, f32[5,3,9,129]{3,1,2,0:T(4,128)S(1)} %get-tuple-element.1464, f32[5,3,9,129]{3,1,2,0:T(4,128)S(1)} %get-tuple-element.1463, f32[5,3,9,129]{3,1,2,0:T(4,128)S(1)} %get-tuple-element.1462, ...), dimensions={1} | concatenate | bytes 1114560 | tf_op jit(solution)/shard_map/concatenate | solution.py:120
  148.1 1.1 fusion.61
  149.4 0.6 copy.89
  (480 shorter events, 11.2 us)
Async XLA Ops:
  0.6 24.6 %copy-start.30 = (f32[3,3]{1,0:T(4,128)S(1)}, f32[3,3]{1,0:T(4,128)}, u32[]{:S(2)}) copy-start(f32[3,3]{1,0:T(4,128)} %constant.423) | copy-start | bytes 112
  0.6 24.6 %copy-start.31 = (f32[3,3]{1,0:T(4,128)S(1)}, f32[3,3]{1,0:T(4,128)}, u32[]{:S(2)}) copy-start(f32[3,3]{1,0:T(4,128)} %constant.424) | copy-start | bytes 112
  0.7 24.6 %copy-start.32 = (f32[3,3]{1,0:T(4,128)S(1)}, f32[3,3]{1,0:T(4,128)}, u32[]{:S(2)}) copy-start(f32[3,3]{1,0:T(4,128)} %constant.425) | copy-start | bytes 112
  0.7 24.6 %copy-start.33 = (f32[3,3]{1,0:T(4,128)S(1)}, f32[3,3]{1,0:T(4,128)}, u32[]{:S(2)}) copy-start(f32[3,3]{1,0:T(4,128)} %constant.426) | copy-start | bytes 112
  4.0 12.3 %collective-permute-start = (f32[1,8,128]{2,1,0:T(8,128)S(1)}, f32[1,8,128]{2,1,0:T(8,128)S(1)}, u32[]{:S(2)}, u32[]{:S(2)}) collective-permute-start(f32[1,8,128]{2,1,0:T(8,128)S(1)} %slice.1784), channel_id=1, source_target_pairs={{0,1},{2,3},{4,5},{6,7},{8,9},{10,11},{12,13},{14,15},{16,17},{18,... | collective-permute-start | bytes 12296 | tf_op jit(solution)/shard_map/ppermute | solution.py:19
  8.9 11.2 %collective-permute-start.2 = (f32[4,3,1,128]{3,1,2,0:T(4,128)S(1)}, f32[4,3,1,128]{3,1,2,0:T(4,128)S(1)}, u32[]{:S(2)}, u32[]{:S(2)}) collective-permute-start(f32[4,3,1,128]{3,1,2,0:T(4,128)S(1)} %copy.124), channel_id=1, source_target_pairs={{0,2},{2,4},{4,6},{6,8},{8,10},{10,12},{12,14},{14,16},{16,18},{18... | collective-permute-start | bytes 18440 | tf_op jit(solution)/shard_map/ppermute | solution.py:29
  12.9 8.0 %collective-permute-start.3 = (f32[4,3,1,128]{3,1,2,0:T(4,128)S(1)}, f32[4,3,1,128]{3,1,2,0:T(4,128)S(1)}, u32[]{:S(2)}, u32[]{:S(2)}) collective-permute-start(f32[4,3,1,128]{3,1,2,0:T(4,128)S(1)} %copy.125), channel_id=1, source_target_pairs={{2,0},{4,2},{6,4},{8,6},{10,8},{12,10},{14,12},{16,14},{18,16},{20... | collective-permute-start | bytes 18440 | tf_op jit(solution)/shard_map/ppermute | solution.py:30
  15.5 10.1 %copy-start.14 = (f32[4,8,128]{2,1,0:T(8,128)}, f32[4,8,128]{2,1,0:T(8,128)S(1)}, u32[]{:S(2)}) copy-start(f32[4,8,128]{2,1,0:T(8,128)S(1)} %subtract_convert_fusion) | copy-start | bytes 49156
  15.5 10.0 %copy-start.35 = (f32[3]{0:T(128)S(1)}, f32[3]{0:T(128)}, u32[]{:S(2)}) copy-start(f32[3]{0:T(128)} %constant.431) | copy-start | bytes 40
  16.4 7.8 %collective-permute-start.1 = (f32[5,1,128]{2,1,0:T(1,128)S(1)}, f32[5,1,128]{2,1,0:T(1,128)S(1)}, u32[]{:S(2)}, u32[]{:S(2)}) collective-permute-start(f32[5,1,128]{2,1,0:T(1,128)S(1)} %fusion.83), channel_id=1, source_target_pairs={{0,2},{2,4},{4,6},{6,8},{8,10},{10,12},{12,14},{14,16},{16,18},{18... | collective-permute-start | bytes 7688 | tf_op jit(solution)/shard_map/ppermute | solution.py:19
  21.5 18.3 %collective-permute-start.4 = (f32[1,3,10,128]{3,1,2,0:T(4,128)}, f32[1,3,10,128]{3,1,2,0:T(4,128)S(1)}, u32[]{:S(2)}, u32[]{:S(2)}) collective-permute-start(f32[1,3,10,128]{3,1,2,0:T(4,128)} %get-tuple-element.1534), channel_id=1, source_target_pairs={{0,1},{2,3},{4,5},{6,7},{8,9},{10,11},{12,13},{14,15},{16,17},{18,... | collective-permute-start | bytes 46088 | tf_op jit(solution)/shard_map/ppermute | solution.py:29
  22.8 17.0 %collective-permute-start.5 = (f32[1,3,10,128]{3,1,2,0:T(4,128)}, f32[1,3,10,128]{3,1,2,0:T(4,128)}, u32[]{:S(2)}, u32[]{:S(2)}) collective-permute-start(f32[1,3,10,128]{3,1,2,0:T(4,128)} %get-tuple-element.1535), channel_id=1, source_target_pairs={{1,0},{3,2},{5,4},{7,6},{9,8},{11,10},{13,12},{15,14},{17,16},{19,... | collective-permute-start | bytes 46088 | tf_op jit(solution)/shard_map/ppermute | solution.py:30
  32.4 0.8 copy-start.27
  32.4 0.8 copy-start.28
  33.2 1.4 copy-start.7
  33.2 1.4 copy-start.9
  34.5 20.9 %collective-permute-start.6 = (f32[3,3,3,8,128]{4,3,2,0,1:T(8,128)}, f32[3,3,3,8,128]{4,3,2,0,1:T(8,128)}, u32[]{:S(2)}, u32[]{:S(2)}) collective-permute-start(f32[3,3,3,8,128]{4,3,2,0,1:T(8,128)} %fusion.66), channel_id=1, source_target_pairs={{0,1},{2,3},{4,5},{6,7},{8,9},{10,11},{12,13},{14,15},{16,17},{18,... | collective-permute-start | bytes 331784 | tf_op jit(solution)/shard_map/while/body/eval_jaxpr/ppermute | solution.py:19
  51.5 1.8 %copy-start.11 = (f32[4,3,8,128]{3,2,1,0:T(8,128)S(1)}, f32[4,3,8,128]{3,2,1,0:T(8,128)}, u32[]{:S(2)}) copy-start(f32[4,3,8,128]{3,2,1,0:T(8,128)} %param.42) | copy-start | bytes 147460
  51.5 1.8 %copy-start.15 = (f32[4,8,128]{2,1,0:T(8,128)S(1)}, f32[4,8,128]{2,1,0:T(8,128)}, u32[]{:S(2)}) copy-start(f32[4,8,128]{2,1,0:T(8,128)} %copy-done.14) | copy-start | bytes 49156
  53.3 0.8 copy-start.5
  54.1 0.8 copy-start.4
  54.9 1.4 copy-start.18
  54.9 1.4 copy-start.19
  54.9 1.4 copy-start.20
  54.9 1.4 copy-start.21
  54.9 1.4 copy-start.22
  54.9 1.4 copy-start.23
  55.4 1.2 copy-start.8
  55.4 1.2 copy-start.10
  56.5 4.7 %copy-start.24 = (f32[3,3,8,128]{3,2,1,0:T(8,128)S(1)}, f32[3,3,8,128]{3,2,1,0:T(8,128)}, u32[]{:S(2)}) copy-start(f32[3,3,8,128]{3,2,1,0:T(8,128)} %get-tuple-element.1453) | copy-start | bytes 110596
  56.5 4.7 %copy-start.25 = (f32[3,3,8,128]{3,2,1,0:T(8,128)S(1)}, f32[3,3,8,128]{3,2,1,0:T(8,128)}, u32[]{:S(2)}) copy-start(f32[3,3,8,128]{3,2,1,0:T(8,128)} %get-tuple-element.1454) | copy-start | bytes 110596
  56.5 4.7 %copy-start.26 = (f32[3,3,8,128]{3,2,1,0:T(8,128)S(1)}, f32[3,3,8,128]{3,2,1,0:T(8,128)}, u32[]{:S(2)}) copy-start(f32[3,3,8,128]{3,2,1,0:T(8,128)} %get-tuple-element.1455) | copy-start | bytes 110596
  57.3 17.0 %copy-start.2 = (f32[3,3,3,8,128]{4,3,2,0,1:T(8,128)}, f32[3,3,3,8,128]{4,3,2,0,1:T(8,128)S(1)}, u32[]{:S(2)}) copy-start(f32[3,3,3,8,128]{4,3,2,0,1:T(8,128)S(1)} %multiply_add_fusion.7) | copy-start | bytes 331780
  74.2 1.0 copy-start.34
  74.3 1.0 copy-start.17
  75.4 20.0 %copy-start = (f32[4,3,8,128]{3,1,2,0:T(4,128)}, f32[4,3,8,128]{3,1,2,0:T(4,128)S(1)}, u32[]{:S(2)}) copy-start(f32[4,3,8,128]{3,1,2,0:T(4,128)S(1)} %copy_add_fusion.1) | copy-start | bytes 147460
  75.4 9.1 %collective-permute-start.7 = (f32[4,3,1,128]{3,1,2,0:T(4,128)S(1)}, f32[4,3,1,128]{3,1,2,0:T(4,128)S(1)}, u32[]{:S(2)}, u32[]{:S(2)}) collective-permute-start(f32[4,3,1,128]{3,1,2,0:T(4,128)S(1)} %get-tuple-element.1538), channel_id=1, source_target_pairs={{0,2},{2,4},{4,6},{6,8},{8,10},{10,12},{12,14},{14,16},{16,18},{18... | collective-permute-start | bytes 18440 | tf_op jit(solution)/shard_map/ppermute | solution.py:29
  82.6 5.0 %collective-permute-start.8 = (f32[4,3,1,128]{3,1,2,0:T(4,128)S(1)}, f32[4,3,1,128]{3,1,2,0:T(4,128)S(1)}, u32[]{:S(2)}, u32[]{:S(2)}) collective-permute-start(f32[4,3,1,128]{3,1,2,0:T(4,128)S(1)} %get-tuple-element.1539), channel_id=1, source_target_pairs={{2,0},{4,2},{6,4},{8,6},{10,8},{12,10},{14,12},{16,14},{18,16},{20... | collective-permute-start | bytes 18440 | tf_op jit(solution)/shard_map/ppermute | solution.py:30
  87.6 5.3 %collective-permute-start.10 = (f32[1,3,10,128]{3,1,2,0:T(4,128)S(1)}, f32[1,3,10,128]{3,1,2,0:T(4,128)S(1)}, u32[]{:S(2)}, u32[]{:S(2)}) collective-permute-start(f32[1,3,10,128]{3,1,2,0:T(4,128)S(1)} %get-tuple-element.1533), channel_id=1, source_target_pairs={{1,0},{3,2},{5,4},{7,6},{9,8},{11,10},{13,12},{15,14},{17,16},{19,... | collective-permute-start | bytes 46088 | tf_op jit(solution)/shard_map/ppermute | solution.py:30
  88.9 4.9 %collective-permute-start.9 = (f32[1,3,10,128]{3,1,2,0:T(4,128)S(1)}, f32[1,3,10,128]{3,1,2,0:T(4,128)S(1)}, u32[]{:S(2)}, u32[]{:S(2)}) collective-permute-start(f32[1,3,10,128]{3,1,2,0:T(4,128)S(1)} %get-tuple-element.1532), channel_id=1, source_target_pairs={{0,1},{2,3},{4,5},{6,7},{8,9},{10,11},{12,13},{14,15},{16,17},{18,... | collective-permute-start | bytes 46088 | tf_op jit(solution)/shard_map/ppermute | solution.py:29
  95.4 14.2 %copy-start.29 = (f32[24,24,1,1]{1,0,3,2:T(8,128)S(1)}, f32[24,24,1,1]{1,0,3,2:T(8,128)}, u32[]{:S(2)}) copy-start(f32[24,24,1,1]{1,0,3,2:T(8,128)} %constant.436) | copy-start | bytes 6916
  109.6 2.3 %copy-start.12 = (f32[4,3,8,128]{3,2,1,0:T(8,128)S(1)}, f32[4,3,8,128]{3,2,1,0:T(8,128)}, u32[]{:S(2)}) copy-start(f32[4,3,8,128]{3,2,1,0:T(8,128)} %param.42) | copy-start | bytes 147460
  109.6 2.3 %copy-start.16 = (f32[4,8,128]{2,1,0:T(8,128)S(1)}, f32[4,8,128]{2,1,0:T(8,128)}, u32[]{:S(2)}) copy-start(f32[4,8,128]{2,1,0:T(8,128)} %copy-done.14) | copy-start | bytes 49156
  112.0 0.9 copy-start.6
  125.2 0.9 copy-start.3
  125.3 1.8 %copy-start.1 = (f32[4,3,8,128]{3,1,2,0:T(4,128)S(1)}, f32[4,3,8,128]{3,1,2,0:T(4,128)}, u32[]{:S(2)}) copy-start(f32[4,3,8,128]{3,1,2,0:T(4,128)} %copy-done) | copy-start | bytes 147460
  127.1 7.0 %collective-permute-start.11 = (f32[4,3,1,128]{3,1,2,0:T(4,128)S(1)}, f32[4,3,1,128]{3,1,2,0:T(4,128)S(1)}, u32[]{:S(2)}, u32[]{:S(2)}) collective-permute-start(f32[4,3,1,128]{3,1,2,0:T(4,128)S(1)} %get-tuple-element.1536), channel_id=1, source_target_pairs={{0,2},{2,4},{4,6},{6,8},{8,10},{10,12},{12,14},{14,16},{16,18},{18... | collective-permute-start | bytes 18440 | tf_op jit(solution)/shard_map/ppermute | solution.py:29
  132.2 5.0 %collective-permute-start.12 = (f32[4,3,1,128]{3,1,2,0:T(4,128)S(1)}, f32[4,3,1,128]{3,1,2,0:T(4,128)S(1)}, u32[]{:S(2)}, u32[]{:S(2)}) collective-permute-start(f32[4,3,1,128]{3,1,2,0:T(4,128)S(1)} %get-tuple-element.1537), channel_id=1, source_target_pairs={{2,0},{4,2},{6,4},{8,6},{10,8},{12,10},{14,12},{16,14},{18,16},{20... | collective-permute-start | bytes 18440 | tf_op jit(solution)/shard_map/ppermute | solution.py:30
  137.2 5.8 %collective-permute-start.13 = (f32[1,3,10,128]{3,1,2,0:T(4,128)S(1)}, f32[1,3,10,128]{3,1,2,0:T(4,128)S(1)}, u32[]{:S(2)}, u32[]{:S(2)}) collective-permute-start(f32[1,3,10,128]{3,1,2,0:T(4,128)S(1)} %get-tuple-element.1530), channel_id=1, source_target_pairs={{0,1},{2,3},{4,5},{6,7},{8,9},{10,11},{12,13},{14,15},{16,17},{18,... | collective-permute-start | bytes 46088 | tf_op jit(solution)/shard_map/ppermute | solution.py:29
  140.9 4.5 %collective-permute-start.14 = (f32[1,3,10,128]{3,1,2,0:T(4,128)S(1)}, f32[1,3,10,128]{3,1,2,0:T(4,128)S(1)}, u32[]{:S(2)}, u32[]{:S(2)}) collective-permute-start(f32[1,3,10,128]{3,1,2,0:T(4,128)S(1)} %get-tuple-element.1531), channel_id=1, source_target_pairs={{1,0},{3,2},{5,4},{7,6},{9,8},{11,10},{13,12},{15,14},{17,16},{19,... | collective-permute-start | bytes 46088 | tf_op jit(solution)/shard_map/ppermute | solution.py:30
  148.1 1.1 copy-start.13
where the time goes:
time: 153 us; the launch traced here: 150 us
  starting transfers between devices  47.8 us (31%)
  local copies, waits for them, and re-layouts  41.6 us (27%)
  blocking collectives  24.6 us (16%)
  other arithmetic  16.8 us (11%)
  waiting for transfers between devices  9.37 us (6%)
  matrix products  5.15 us (3%)
  loops' own time  2.64 us (2%)
  between operations  2.09 us (1%)
    concatenate x3, local copies, waits for them, and re-layouts, element_forces(): stacked = jnp.concatenate(pieces, axis=1)  25.4 us
    ppermute x6, starting transfers between devices, extended_2(): before = lax.ppermute(last, axis, up)  25.2 us
    all_gather x6, blocking collectives, carried_in(): gathered = jax.tree.map(lambda a: lax.all_gather(a, axis), part)  24.6 us
    ppermute x3, starting transfers between devices, passed_along(): return lax.ppermute(block, axis, route)  12.8 us
    ppermute x6, starting transfers between devices, extended_2(): after = lax.ppermute(leading, axis, down)  9.82 us
    ppermute x6, waiting for transfers between devices, extended_2(): after = lax.ppermute(leading, axis, down)  8.49 us
    dot_general x3, matrix products, element_forces(): jnp.einsum('ij,zjxy->zixy', stiffness, stacked, precision=lax.Precision.H...  5.15 us
    mul x107, local copies, waits for them, and re-layouts, apply(): product = left * other[entry]  4.28 us
  transfers between devices with their start and end apart: 15, of which 4 were waited for; matrix products, arithmetic and copies ran while one was open for 18% of the time, Pallas kernels for 0%

commit v1 on v0

v1 whole, which is shorter than its diff:
```python
import functools
import math

import jax
import jax.numpy as jnp
import numpy as np
from jax import lax
from jax.experimental import pallas as pl
from jax.experimental.pallas import tpu as pltpu
from jax.sharding import PartitionSpec as P

SWEEPS = 2
MESH = pl.DeviceIdType.MESH

relax_shifts = (0.0, 0.05, 0.2)
relax_weights = (0.5, 0.3, 0.2)


def element_matrix():
    spacing = np.array([1.0, 8.0, 8.0])
    poisson = 0.3
    lame_first = poisson / ((1.0 + poisson) * (1.0 - 2.0 * poisson))
    lame_second = 0.5 / (1.0 + poisson)
    elastic = np.zeros((6, 6))
    elastic[:3, :3] = lame_first
    for entry in range(3):
        elastic[entry, entry] += 2.0 * lame_second
        elastic[3 + entry, 3 + entry] = lame_second
    points = (0.5 - 0.5 / math.sqrt(3.0), 0.5 + 0.5 / math.sqrt(3.0))
    matrix = np.zeros((24, 24))
    volume = float(np.prod(spacing)) / 8.0
    for point_z in points:
        for point_x in points:
            for point_y in points:
                position = (point_z, point_x, point_y)
                strain = np.zeros((6, 24))
                for corner in range(8):
                    upper_side = (corner >> 2 & 1, corner >> 1 & 1, corner & 1)
                    values = [
                        position[direction] if upper_side[direction] else 1.0 - position[direction]
                        for direction in range(3)
                    ]
                    slopes = [
                        (1.0 if upper_side[direction] else -1.0) / spacing[direction]
                        for direction in range(3)
                    ]
                    gradient = [
                        slopes[0] * values[1] * values[2],
                        values[0] * slopes[1] * values[2],
                        values[0] * values[1] * slopes[2],
                    ]
                    column = 3 * corner
                    strain[0, column] = gradient[0]
                    strain[1, column + 1] = gradient[1]
                    strain[2, column + 2] = gradient[2]
                    strain[3, column] = gradient[1]
                    strain[3, column + 1] = gradient[0]
                    strain[4, column + 1] = gradient[2]
                    strain[4, column + 2] = gradient[1]
                    strain[5, column] = gradient[2]
                    strain[5, column + 2] = gradient[0]
                matrix += strain.T @ elastic @ strain * volume
    largest = 0.0
    for entry in range(24):
        largest = largest if largest >= float(matrix[entry, entry]) else float(matrix[entry, entry])
    return matrix / largest


def parity_blocks():
    pair = np.array([[1.0, 1.0], [-1.0, 1.0]])
    modes = np.kron(np.kron(np.kron(pair, pair), pair), np.eye(3))
    matrix = modes @ element_matrix() @ modes.T / 64.0
    terms = {}
    for parity in range(8):
        index = [3 * (parity ^ (4 >> comp)) + comp for comp in range(3)]
        for row in index:
            terms[divmod(row, 3)] = [
                (divmod(col, 3), float(matrix[row, col]))
                for col in index
                if abs(matrix[row, col]) > 1e-12
            ]
    return terms


def total(values):
    values = list(values)
    while len(values) > 1:
        paired = [a + b for a, b in zip(values[::2], values[1::2])]
        values = paired + values[len(values) - len(values) % 2 :]
    return values[0]


def kernel(
    layers, tiles, loads, guess, material, clamped, moduli, distortion, imbalance,
    mat_buf, cl_buf, u0_buf, r_buf, m_buf, free_buf, du_buf, fac_buf, y_buf,
    send_sem, recv_sem, u_send_sem, u_recv_sem,
):
    depth, comps, rows, lanes = loads.shape
    height = depth * layers
    wide = 2 * rows
    build = lax.axis_index("build")
    tile = lax.axis_index("tile")
    base = build * depth
    has = {-1: tile > 0, 0: None, 1: tile < tiles - 1}
    z_has = {-1: build > 0, 0: None, 1: build < layers - 1}
    stiff = element_matrix()
    terms = parity_blocks()

    def when(condition, run):
        if condition is None:
            run()
        else:
            pl.when(condition)(run)

    halo = pl.ds(rows, rows)
    mat_buf[:, halo] = jnp.zeros((height, rows, lanes), jnp.int32)
    cl_buf[:, halo] = jnp.ones((height, rows, lanes), jnp.int32)
    u0_buf[...] = jnp.zeros(u0_buf.shape, jnp.float32)
    r_buf[:, :, halo] = jnp.zeros((height, comps, rows, lanes), jnp.float32)

    barrier = pltpu.get_barrier_semaphore()
    peers = [(side, offset) for offset in range(layers) for side in (0, 1, -1) if side or offset]

    def device(side, offset):
        return {"tile": tile + side, "build": lax.rem(build + offset, layers)}

    for side, offset in peers:
        def greet(side=side, offset=offset):
            pl.semaphore_signal(barrier, inc=1, device_id=device(side, offset), device_id_type=MESH)
        when(has[side], greet)
    sides = has[-1].astype(jnp.int32) + has[1].astype(jnp.int32)
    pl.semaphore_wait(barrier, layers - 1 + layers * sides)

    def spans(side, before, after):
        if side == 0:
            return pl.ds(0, rows), pl.ds(0, rows)
        if side == 1:
            return pl.ds(rows - before, before), pl.ds(wide - before, before)
        return pl.ds(0, after), pl.ds(rows, after)

    def slab_copy(kind, side, offset, source_build):
        before, after = ((3, 2), (2, 2), (2, 2))[kind]
        take, put = spans(side, before, after)
        here = pl.ds(base, depth)
        there = pl.ds(source_build * depth, depth)
        if kind == 2:
            source, target = r_buf.at[here, :, take], r_buf.at[there, :, put]
        else:
            operand, buffer = ((material, mat_buf), (clamped, cl_buf))[kind]
            source, target = operand.at[:, take], buffer.at[there, put]
        return pltpu.make_async_remote_copy(
            src_ref=source, dst_ref=target,
            send_sem=send_sem.at[kind, side + 1, offset],
            recv_sem=recv_sem.at[kind, side + 1, offset],
            device_id=device(side, offset), device_id_type=MESH,
        )

    def each_slab(kind, act):
        for side, offset in peers:
            def run(side=side, offset=offset):
                act(kind, side, offset)
            when(has[-side if act is slab_arrive else side] if side else None, run)

    def slab_start(kind, side, offset):
        slab_copy(kind, side, offset, build).start()

    def slab_sent(kind, side, offset):
        slab_copy(kind, side, offset, build).wait_send()

    def slab_arrive(kind, side, offset):
        slab_copy(kind, side, offset, lax.rem(build + layers - offset, layers)).wait_recv()

    def u0_copy(side, step):
        take, put = spans(side, 1, 1)
        from_z, to_z = {0: (pl.ds(0, depth), pl.ds(1, depth)),
                        1: (pl.ds(depth - 1, 1), pl.ds(0, 1)),
                        -1: (pl.ds(0, 1), pl.ds(depth + 1, 1))}[step]
        return pltpu.make_async_remote_copy(
            src_ref=guess.at[from_z, :, take], dst_ref=u0_buf.at[to_z, :, put],
            send_sem=u_send_sem.at[step + 1, side + 1], recv_sem=u_recv_sem.at[step + 1, side + 1],
            device_id={"tile": tile + side, "build": build + step}, device_id_type=MESH,
        )

    def each_u0(act, sign):
        for step in (1, -1, 0):
            for side in (0, 1, -1):
                if step or side:
                    conditions = [c for c in (has[sign * side], z_has[sign * step]) if c is not None]
                    condition = functools.reduce(jnp.logical_and, conditions)
                    def run(side=side, step=step):
                        act(u0_copy(side, step))
                    when(condition, run)

    each_u0(lambda copy: copy.start(), 1)
    each_slab(0, slab_start)
    each_slab(1, slab_start)

    own = pl.ds(0, rows)
    u0_buf[1 : depth + 1, :, own] = guess[...]
    mat_buf[pl.ds(base, depth), own] = material[...]
    cl_buf[pl.ds(base, depth), own] = clamped[...]
    edge = jnp.zeros((comps, wide, lanes), jnp.float32)
    m_buf[0] = edge[0]
    du_buf[0] = edge
    du_buf[height + 1] = edge

    lane = lax.broadcasted_iota(jnp.int32, (wide, lanes), 1)
    row = lax.broadcasted_iota(jnp.int32, (wide, lanes), 0)
    inside_next = lane < lanes - 1
    inside_prev = lane > 0
    before_first = (row >= wide - 3) & (tile == 0)

    def y_next(a):
        return jnp.where(inside_next, pltpu.roll(a, lanes - 1, 1), 0.0)

    def y_prev(a):
        return jnp.where(inside_prev, pltpu.roll(a, 1, 1), 0.0)

    def x_next(a):
        return pltpu.roll(a, wide - 1, 0)

    def x_prev(a):
        return pltpu.roll(a, 1, 0)

    def plane_modes(u):
        out = []
        for comp in range(3):
            ahead = y_next(u[comp])
            both = (u[comp] + ahead, ahead - u[comp])
            steps = [x_next(b) for b in both]
            out.append([both[0] + steps[0], both[1] + steps[1], steps[0] - both[0], steps[1] - both[1]])
        return out

    def element(lower, upper, m):
        modes = {}
        for comp in range(3):
            for h in range(4):
                modes[h, comp] = lower[comp][h] + upper[comp][h]
                modes[4 + h, comp] = upper[comp][h] - lower[comp][h]
        force = {}
        for key, parts in terms.items():
            force[key] = m * total(modes[other] * weight for other, weight in parts) if parts else None
        low, high = [], []
        for comp in range(3):
            low.append([])
            high.append([])
            for h in range(4):
                even, odd = force[h, comp], force[4 + h, comp]
                if even is None:
                    low[comp].append(-odd)
                    high[comp].append(odd)
                elif odd is None:
                    low[comp].append(even)
                    high[comp].append(even)
                else:
                    low[comp].append(even - odd)
                    high[comp].append(even + odd)
        return low, high

    def node_force(f):
        out = []
        for comp in range(3):
            even = (f[comp][0] - f[comp][2]) + x_prev(f[comp][0] + f[comp][2])
            odd = (f[comp][1] - f[comp][3]) + x_prev(f[comp][1] + f[comp][3])
            out.append((even - odd) + y_prev(even + odd))
        return out

    def added(a, b):
        return [[p + q for p, q in zip(s, t)] for s, t in zip(a, b)]

    def planes(ref, index):
        return [ref[index, comp] for comp in range(3)]

    def layer_force(field, first, m_first, lower, held):
        upper = plane_modes(planes(field, first + 1))
        low, high = element(lower, upper, m_buf[m_first])
        return node_force(added(low, held)), upper, high

    blank = jnp.zeros((wide, lanes), jnp.float32)
    nothing = [[blank] * 4 for _ in range(3)]

    each_u0(lambda copy: copy.wait_recv(), -1)
    each_slab(0, slab_arrive)
    support, part = moduli[0], moduli[1]

    def fill_modulus(k, carry):
        m = jnp.where(mat_buf[k] == 1, part, support)
        m_buf[k + 1] = jnp.where(before_first, 0.0, m)
        return carry

    lax.fori_loop(0, height, fill_modulus, 0)

    def first_residual(k, carry):
        lower, held = carry
        force, upper, high = layer_force(u0_buf, k + 1, base + k + 1, lower, held)
        is_free = clamped[k] == 0
        for comp in range(3):
            r_buf[base + k, comp, own] = jnp.where(is_free, loads[k, comp] - force[comp][:rows], 0.0)
        return upper, high

    start = plane_modes(planes(u0_buf, 0))
    lower = plane_modes(planes(u0_buf, 1))
    unused, held = element(start, lower, m_buf[base])
    lax.fori_loop(0, depth, first_residual, (lower, held))
    each_slab(2, slab_start)
    each_slab(1, slab_arrive)

    def fill_free(k, carry):
        free_buf[k] = 1.0 - cl_buf[k].astype(jnp.float32)
        return carry

    lax.fori_loop(0, height, fill_free, 0)
    free_buf[height] = blank

    kzz, kxx, kyy = (float(stiff[c, c]) for c in range(3))
    kzx, kzy, kxy = float(stiff[0, 1]), float(stiff[0, 2]), float(stiff[1, 2])
    uzz, uxx, uyy = (float(stiff[c, 12 + c]) for c in range(3))
    uzx, uzy, uxy = -float(stiff[0, 13]), -float(stiff[0, 14]), float(stiff[1, 14])
    uxz, uyz = -float(stiff[1, 12]), -float(stiff[2, 12])
    pairs = ((0, 0), (0, 1), (0, 2), (1, 1), (1, 2), (2, 2))

    def corner_sums(m):
        behind = y_prev(m)
        plus, minus = m + behind, behind - m
        plus_b, minus_b = x_prev(plus), x_prev(minus)
        return plus + plus_b, plus_b - plus, minus + minus_b, minus_b - minus

    def factor(k, carry):
        sums_below, schur = carry
        sums = corner_sums(m_buf[k + 1])
        free = free_buf[k]
        is_free = free > 0.5
        next_free = free * free_buf[k + 1]
        s, sx, sy, sxy = [a + b for a, b in zip(sums, (sums_below[0], -sums_below[1], -sums_below[2], sums_below[3]))]
        diagonal = {
            (0, 0): jnp.where(is_free, kzz * s, 1.0), (1, 1): jnp.where(is_free, kxx * s, 1.0),
            (2, 2): jnp.where(is_free, kyy * s, 1.0), (0, 1): free * (-kzx * sx),
            (0, 2): free * (-kzy * sy), (1, 2): free * (kxy * sxy),
        }
        t, tx, ty, txy = [next_free * a for a in sums]
        up = [
            [uzz * t, uzx * tx, uzy * ty],
            [uxz * tx, uxx * t, uxy * txy],
            [uyz * ty, uxy * txy, uyy * t],
        ]
        following = []
        for shift in range(len(relax_shifts)):
            scale = 1.0 + relax_shifts[shift]
            a = {}
            for at, (p, q) in enumerate(pairs):
                d = diagonal[p, q] if scale == 1.0 else scale * diagonal[p, q]
                a[p, q] = a[q, p] = d - schur[shift][at]
            c00 = a[1, 1] * a[2, 2] - a[1, 2] * a[1, 2]
            c01 = a[1, 2] * a[0, 2] - a[0, 1] * a[2, 2]
            c02 = a[0, 1] * a[1, 2] - a[1, 1] * a[0, 2]
            c11 = a[0, 0] * a[2, 2] - a[0, 2] * a[0, 2]
            c12 = a[0, 1] * a[0, 2] - a[0, 0] * a[1, 2]
            c22 = a[0, 0] * a[1, 1] - a[0, 1] * a[0, 1]
            inverse_det = 1.0 / (a[0, 0] * c00 + a[0, 1] * c01 + a[0, 2] * c02)
            w = {}
            for at, ((p, q), c) in enumerate(zip(pairs, (c00, c01, c02, c11, c12, c22))):
                w[p, q] = w[q, p] = c * inverse_det
                fac_buf[k, shift, at] = w[p, q]
            couple = [[w[p, 0] * up[0][q] + w[p, 1] * up[1][q] + w[p, 2] * up[2][q] for q in range(3)] for p in range(3)]
            for p in range(3):
                for q in range(3):
                    fac_buf[k, shift, 6 + 3 * p + q] = couple[p][q]
            following.append([
                up[0][p] * couple[0][q] + up[1][p] * couple[1][q] + up[2][p] * couple[2][q] for p, q in pairs
            ])
        return list(sums), following

    count = len(relax_shifts)
    lax.fori_loop(0, height, factor, ([blank] * 4, [[blank] * 6 for _ in range(count)]))

    each_slab(2, slab_arrive)

    def eliminate(k, residual, y_below):
        out = []
        for shift in range(count):
            y = [residual[comp] - y_below[shift][comp] for comp in range(3)]
            for comp in range(3):
                y_buf[k, shift, comp] = y[comp]
            out.append([
                total(fac_buf[k, shift, 6 + 3 * p + q] * y[p] for p in range(3)) for q in range(3)
            ])
        return out

    no_y = [[blank] * 3 for _ in range(count)]
    spots = {pair: at for at, pair in enumerate(pairs)}

    def back(first):
        def step(i, x_above):
            k = height - 1 - i
            solved, change = [], [None] * 3
            for shift in range(count):
                y = [y_buf[k, shift, comp] for comp in range(3)]
                w = [fac_buf[k, shift, at] for at in range(6)]
                x = []
                for p in range(3):
                    own_part = total(w[spots[min(p, q), max(p, q)]] * y[q] for q in range(3))
                    above = total(fac_buf[k, shift, 6 + 3 * p + q] * x_above[shift][q] for q in range(3))
                    x.append(own_part - above)
                    term = relax_weights[shift] * x[p]
                    change[p] = term if change[p] is None else change[p] + term
                solved.append(x)
            for comp in range(3):
                du_buf[k + 1, comp] = change[comp] if first else du_buf[k + 1, comp] + change[comp]
            return solved

        lax.fori_loop(0, height, step, no_y)

    def forward_first(k, y_below):
        return eliminate(k, planes(r_buf, k), y_below)

    def forward_next(k, carry):
        lower, held, y_below = carry
        force, upper, high = layer_force(du_buf, k + 1, k + 1, lower, held)
        free = free_buf[k]
        residual = [r_buf[k, comp] - free * force[comp] for comp in range(3)]
        return upper, high, eliminate(k, residual, y_below)

    lax.fori_loop(0, height, forward_first, no_y)
    back(True)
    for sweep in range(1, SWEEPS):
        lax.fori_loop(0, height, forward_next, (plane_modes(planes(du_buf, 1)), nothing, no_y))
        back(False)

    def last_residual(k, carry):
        lower, held = carry
        force, upper, high = layer_force(du_buf, base + k + 1, base + k + 1, lower, held)
        free = free_buf[base + k, own]
        for comp in range(3):
            imbalance[k, comp] = r_buf[base + k, comp, own] - free * force[comp][:rows]
            distortion[k, comp] = guess[k, comp] + du_buf[base + k + 1, comp, own]
        return upper, high

    start = plane_modes(planes(du_buf, base))
    lower = plane_modes(planes(du_buf, base + 1))
    unused, held = element(start, lower, m_buf[base])
    lax.fori_loop(0, depth, last_residual, (lower, held))

    each_u0(lambda copy: copy.wait_send(), 1)
    for kind in range(3):
        each_slab(kind, slab_sent)


def on_device(layers, tiles, loads, guess, material, clamped, moduli):
    depth, comps, rows, lanes = loads.shape
    height, wide, count = depth * layers, 2 * rows, len(relax_shifts)
    f32, i32 = jnp.float32, jnp.int32
    vmem = pl.BlockSpec(memory_space=pltpu.VMEM)
    shape = jax.ShapeDtypeStruct(loads.shape, f32)
    return pl.pallas_call(
        functools.partial(kernel, layers, tiles),
        out_shape=(shape, shape),
        in_specs=[vmem] * 4 + [pl.BlockSpec(memory_space=pltpu.SMEM)],
        out_specs=(vmem, vmem),
        scratch_shapes=[
            pltpu.VMEM((height, wide, lanes), i32),
            pltpu.VMEM((height, wide, lanes), i32),
            pltpu.VMEM((depth + 2, comps, wide, lanes), f32),
            pltpu.VMEM((height, comps, wide, lanes), f32),
            pltpu.VMEM((height + 1, wide, lanes), f32),
            pltpu.VMEM((height + 1, wide, lanes), f32),
            pltpu.VMEM((height + 2, comps, wide, lanes), f32),
            pltpu.VMEM((height, count, 15, wide, lanes), f32),
            pltpu.VMEM((height, count, comps, wide, lanes), f32),
            pltpu.SemaphoreType.DMA((3, 3, layers)),
            pltpu.SemaphoreType.DMA((3, 3, layers)),
            pltpu.SemaphoreType.DMA((3, 3)),
            pltpu.SemaphoreType.DMA((3, 3)),
        ],
        compiler_params=pltpu.CompilerParams(
            collective_id=0, has_side_effects=True, vmem_limit_bytes=40 * 1024 * 1024
        ),
        name="relax",
    )(loads, guess, material, clamped, moduli)


def solution(mesh):
    field, plane = P("build", None, "tile", None), P("build", "tile", None)
    return jax.shard_map(
        functools.partial(on_device, mesh.shape["build"], mesh.shape["tile"]),
        mesh=mesh,
        in_specs=(field, field, plane, plane, P()),
        out_specs=(field, field),
        check_vma=False,
    )
```

time: 153 us -> 21.3 us (0.14); the launches traced: 150 us -> 21 us
  starting transfers between devices: 47.8 us -> 0 us
  local copies, waits for them, and re-layouts: 41.6 us -> 4.92 us
  blocking collectives: 24.6 us -> 0 us
  other arithmetic: 16.8 us -> 0 us
  Pallas kernels: 0 us -> 15.4 us
  waiting for transfers between devices: 9.37 us -> 0 us
  matrix products: 5.15 us -> 0 us
  loops' own time: 2.64 us -> 0 us
    ppermute x15 -> x0, starting transfers between devices: 47.8 us -> none  [the longest x6 25.2 us: extended_2(): before = lax.ppermute(last, axis, up)]
    concatenate x4 -> x0, local copies, waits for them, and re-layouts: 25.4 us -> none  [the longest x3 25.4 us: element_forces(): stacked = jnp.concatenate(pieces, axis=1)]
    all_gather x6 -> x0, blocking collectives: 24.6 us -> none  [carried_in(): gathered = jax.tree.map(lambda a: lax.all_gather(a, axis), part)]
    pallas_call x0 -> x1, Pallas kernels: none -> 15.4 us  [on_device(): pl.pallas_call(functools.partial(kernel, layers, tiles), out_shape=(shape...]
    ppermute x15 -> x0, waiting for transfers between devices: 9.37 us -> none  [the longest x6 8.49 us: extended_2(): after = lax.ppermute(leading, axis, down)]
    sub x45 -> x0, other arithmetic: 6.73 us -> none  [the longest x16 3.53 us: forward(): current = apply(inverse, right_block - apply(below_block, previous))]
    slice x11 -> x0, local copies, waits for them, and re-layouts: 6.43 us -> none  [the longest x3 3.42 us: element_forces(): extended[step_z:step_z + depth + 1, :, step_x:step_x + width + 1, step_y:...]
    dot_general x3 -> x0, matrix products: 5.15 us -> none  [element_forces(): jnp.einsum('ij,zjxy->zixy', stiffness, stacked, precision=lax.Precision.H...]
  transfers between devices with their start and end apart: 15 -> 0, of which waited for: 4 -> 0; matrix products, arithmetic and copies ran while one was open for 18% -> 0% of each run, Pallas kernels for 0% -> 0%
where the time goes in v1:
time: 21.3 us; the launch traced here: 21 us
  Pallas kernels  15.4 us (72%)
  local copies, waits for them, and re-layouts  4.92 us (23%)
  between operations  0.65 us (3%)
    pallas_call x1, Pallas kernels, on_device(): pl.pallas_call(functools.partial(kernel, layers, tiles), out_shape=(shape...  15.4 us
    unnamed x12, local copies, waits for them, and re-layouts  4.92 us

profile of v1, /device:TPU:1, one launch (start us, length us, event | category | flops | bytes accessed | tf_op | source)
XLA Modules:
  0.0 21.0 jit_solution(14600716342292430110)
XLA Ops:
  0.6 0.0 copy-start
  0.6 0.8 %copy-done = f32[4,3,8,128]{3,2,1,0:T(8,128)S(1)} copy-done((f32[4,3,8,128]{3,2,1,0:T(8,128)S(1)}, f32[4,3,8,128]{3,2,1,0:T(8,128)}, u32[]{:S(2)}) %copy-start) | copy-done | bytes 49176
  1.4 0.0 copy-start.1
  1.4 0.8 %copy-done.1 = f32[4,3,8,128]{3,2,1,0:T(8,128)S(1)} copy-done((f32[4,3,8,128]{3,2,1,0:T(8,128)S(1)}, f32[4,3,8,128]{3,2,1,0:T(8,128)}, u32[]{:S(2)}) %copy-start.1) | copy-done | bytes 49176
  2.2 0.0 copy-start.2
  2.2 0.7 %copy-done.2 = s32[4,8,128]{2,1,0:T(8,128)S(1)} copy-done((s32[4,8,128]{2,1,0:T(8,128)S(1)}, s32[4,8,128]{2,1,0:T(8,128)}, u32[]{:S(2)}) %copy-start.2) | copy-done | bytes 16408
  2.9 0.0 copy-start.3
  2.9 0.7 %copy-done.3 = s32[4,8,128]{2,1,0:T(8,128)S(1)} copy-done((s32[4,8,128]{2,1,0:T(8,128)S(1)}, s32[4,8,128]{2,1,0:T(8,128)}, u32[]{:S(2)}) %copy-start.3) | copy-done | bytes 16408
  3.7 0.0 copy-start.4
  3.7 0.7 %copy-done.4 = f32[2]{0:T(128)S(1)} copy-done((f32[2]{0:T(128)S(1)}, f32[2]{0:T(128)}, u32[]{:S(2)}) %copy-start.4) | copy-done | bytes 32
  4.3 15.4 %relax.1 = (f32[4,3,8,128]{3,2,1,0:T(8,128)S(1)}, f32[4,3,8,128]{3,2,1,0:T(8,128)S(1)}) custom-call(f32[4,3,8,128]{3,2,1,0:T(8,128)S(1)} %copy-done, f32[4,3,8,128]{3,2,1,0:T(8,128)S(1)} %copy-done.1, s32[4,8,128]{2,1,0:T(8,128)S(1)} %copy-done.2, s32[4,8,128]{2,1,0:T(8,128)S(1)} %copy-done.3, f32[2]{0:T(128)S(1)} %copy-done.4), custom_call_target="tpu_custom_call" | custom-call | tf_op jit(solution)/shard_map/relax/pallas_call | solution.py:454
  19.7 0.6 %copy.9 = f32[4,3,8,128]{3,2,1,0:T(8,128)} copy(f32[4,3,8,128]{3,2,1,0:T(8,128)S(1)} %get-tuple-element.4) | data formatting | bytes 98304
  20.4 0.6 %copy.10 = f32[4,3,8,128]{3,2,1,0:T(8,128)} copy(f32[4,3,8,128]{3,2,1,0:T(8,128)S(1)} %get-tuple-element.5) | data formatting | bytes 98304
Async XLA Ops:
  0.6 0.8 %copy-start = (f32[4,3,8,128]{3,2,1,0:T(8,128)S(1)}, f32[4,3,8,128]{3,2,1,0:T(8,128)}, u32[]{:S(2)}) copy-start(f32[4,3,8,128]{3,2,1,0:T(8,128)} %loads.1) | copy-start | bytes 147460
  1.4 0.8 %copy-start.1 = (f32[4,3,8,128]{3,2,1,0:T(8,128)S(1)}, f32[4,3,8,128]{3,2,1,0:T(8,128)}, u32[]{:S(2)}) copy-start(f32[4,3,8,128]{3,2,1,0:T(8,128)} %guess.1) | copy-start | bytes 147460
  2.2 0.7 %copy-start.2 = (s32[4,8,128]{2,1,0:T(8,128)S(1)}, s32[4,8,128]{2,1,0:T(8,128)}, u32[]{:S(2)}) copy-start(s32[4,8,128]{2,1,0:T(8,128)} %material.1) | copy-start | bytes 49156
  2.9 0.7 %copy-start.3 = (s32[4,8,128]{2,1,0:T(8,128)S(1)}, s32[4,8,128]{2,1,0:T(8,128)}, u32[]{:S(2)}) copy-start(s32[4,8,128]{2,1,0:T(8,128)} %clamped.1) | copy-start | bytes 49156
  3.7 0.7 %copy-start.4 = (f32[2]{0:T(128)S(1)}, f32[2]{0:T(128)}, u32[]{:S(2)}) copy-start(f32[2]{0:T(128)} %moduli.1) | copy-start | bytes 28
